TPU v7x, 32 devices: a whole 2x2x4 slice. The times are simulated.
32 devices in a mesh: seq: 8 (over y, x, core), chan: 4 (over z).
Axes of the slice: x: 2, y: 2, z: 4, core: 2. Of those that a mesh axis runs over, the one named last changes fastest.
Arguments:
- residual: bfloat16 [1024, 8192], P('seq', 'chan'), may hold values from -64 to 64
- query_in: bfloat16 [1024, 8192], P('seq', 'chan'), may hold values from -6 to 6
- key_in: bfloat16 [1024, 8192], P('seq', 'chan'), may hold values from -6 to 6
- value_in: bfloat16 [1024, 8192], P('seq', 'chan'), may hold values from -6 to 6
- short_filter: float32 [3, 3, 8192], P(None, None, 'chan'), may hold values from -3.5 to 3.5
- decay_rate: float32 [16, 8192], P(None, 'chan'), may hold values from 0 to 1
- residue: float32 [16, 8192], P(None, 'chan'), may hold values from -1.5 to 1.5
- skip_gain: float32 [8192], P('chan'), may hold values from -3 to 3
- norm_gain: float32 [8192], P('chan'), may hold values from 0.1 to 1.9
Outputs:
- residual_out: bfloat16 [1024, 8192], P('seq', 'chan')
- normed: bfloat16 [1024, 8192], P('seq', 'chan')
All inputs are finite; a program needn't handle non-finite values.
Results may differ from a plain program's by a relative error of at most 0.0055.
Values may be sent and summed in bfloat16 or wider, within the bound.
A program may use at most 128 MiB of HBM per device.

v0:
```python
import jax
import jax.numpy as jnp
from jax import lax
from jax.sharding import PartitionSpec as P

D = 8192


sub_block = 16
epsilon = 1e-06
highest = lax.Precision.HIGHEST


def shifted(block, axis, distance):
    devices = range(lax.axis_size(axis))
    route = [(i - distance, i) for i in devices if i - distance in devices]
    return lax.ppermute(block, axis, route)


def short_features(inputs, before, tap_weights):
    lag_rows = before.shape[0]
    token_rows = inputs.shape[0]
    extended = jnp.concatenate([before, inputs], axis=0).astype(jnp.float32)
    result = tap_weights[0][None, :] * extended[lag_rows : lag_rows + token_rows]
    for offset in range(1, lag_rows + 1):
        result = (
            result
            + tap_weights[offset][None, :]
            * extended[lag_rows - offset : lag_rows - offset + token_rows]
        )
    return result


def link_states(earlier, later):
    return (earlier[0] * later[0], later[0] * earlier[1] + later[1])


def body(
    residual, query_in, key_in, value_in, short_filter, decay_rate, residue, skip_gain, norm_gain
):
    token_rows, chan_width = residual.shape
    lag_rows = short_filter.shape[1] - 1
    tail_rows = (
        query_in[token_rows - lag_rows :],
        key_in[token_rows - lag_rows :],
        value_in[token_rows - lag_rows :],
    )
    before = shifted((tail_rows[0], tail_rows[1], tail_rows[2]), "seq", 1)
    query_side = short_features(query_in, before[0], short_filter[0])
    key_side = short_features(key_in, before[1], short_filter[1])
    value_side = short_features(value_in, before[2], short_filter[2])
    mixed = key_side * value_side
    weights = residue * jnp.sqrt(2.0 * decay_rate)
    sub_count = token_rows // sub_block
    positions = jnp.arange(sub_block, dtype=jnp.float32)
    local_taps = jnp.sum(
        weights[None] * jnp.exp(-decay_rate[None] * positions[:, None, None]), axis=1
    )
    lag_table = positions[:, None] - positions[None, :]
    one_hot = (lag_table[:, :, None] == positions[None, None, :]).astype(jnp.float32)
    toeplitz = jnp.dot(
        one_hot.reshape(sub_block * sub_block, sub_block), local_taps, precision=highest
    ).reshape(sub_block, sub_block, chan_width)
    blocks = mixed.reshape(sub_count, sub_block, chan_width)
    inside = jnp.sum(toeplitz[None, :, :, :] * blocks[:, None, :, :], axis=2)
    tail_decay = jnp.exp(-decay_rate[None] * (sub_block - 1.0 - positions)[:, None, None])
    sub_states = jnp.sum(blocks[:, :, None, :] * tail_decay[None], axis=1)
    step_decay = jnp.broadcast_to(jnp.exp(-decay_rate * sub_block)[None], sub_states.shape)
    _, running = lax.associative_scan(link_states, (step_decay, sub_states), axis=0)
    block_state = running[sub_count - 1]
    entering = jnp.concatenate([jnp.zeros_like(running[:1]), running[:-1]], axis=0)
    position = lax.axis_index("seq")
    piece = lax.all_gather(
        block_state[None].astype(jnp.bfloat16), "seq", axis=0, tiled=True
    ).astype(jnp.float32)
    members = piece.shape[0]
    sources = jnp.arange(members, dtype=jnp.int32)
    distance = position - 1 - sources
    spans = (token_rows * jnp.maximum(distance, 0)).astype(jnp.float32)
    factors = jnp.exp(-decay_rate[None] * spans[:, None, None])
    masked = jnp.where((distance >= 0)[:, None, None], factors * piece, 0.0)
    carried = jnp.zeros_like(block_state) + jnp.sum(masked, axis=0)
    sub_starts = jnp.arange(sub_count, dtype=jnp.float32) * sub_block
    entering = entering + jnp.exp(-decay_rate[None] * sub_starts[:, None, None]) * carried[None]
    readout = weights[None] * jnp.exp(-decay_rate[None] * (positions + 1.0)[:, None, None])
    across = jnp.sum(readout[None, :, :, :] * entering[:, None, :, :], axis=2)
    convolved = (inside + across).reshape(token_rows, chan_width)
    gated = query_side * (convolved + skip_gain[None, :] * mixed)
    summed = (residual.astype(jnp.float32) + gated).astype(jnp.bfloat16)
    widened = lax.optimization_barrier(summed).astype(jnp.float32)
    row_squares = lax.psum(jnp.sum(widened * widened, axis=1), "chan")
    inverse_rms = lax.rsqrt(row_squares / D + epsilon)
    normed = (widened * inverse_rms[:, None] * norm_gain[None, :]).astype(jnp.bfloat16)
    return (summed, normed)


def solution(mesh):
    in_specs = (
        P("seq", "chan"),
        P("seq", "chan"),
        P("seq", "chan"),
        P("seq", "chan"),
        P(None, None, "chan"),
        P(None, "chan"),
        P(None, "chan"),
        P("chan"),
        P("chan"),
    )
    out_specs = (P("seq", "chan"), P("seq", "chan"))
    return jax.shard_map(body, mesh=mesh, in_specs=in_specs, out_specs=out_specs, check_vma=False)
```

profile of v0, /device:TPU:0, one launch (start us, length us, event | category | flops | bytes accessed | tf_op | source)
XLA Modules:
  0.0 87.4 jit_solution(9873750867871686147)
XLA Ops:
  0.6 0.8 slice.156
  1.4 2.4 %collective-permute-start.1 = (bf16[2,2048]{1,0:T(2,128)(2,1)S(1)}, bf16[2,2048]{1,0:T(2,128)(2,1)S(1)}, u32[]{:S(2)}, u32[]{:S(2)}) collective-permute-start(bf16[2,2048]{1,0:T(2,128)(2,1)S(1)} %slice.156), channel_id=1, source_target_pairs={{0,4},{4,8},{8,12},{12,16},{16,20},{20,24},{24,28},{1,5},{5,9},{9,... | collective-permute-start | bytes 24584 | tf_op jit(solution)/shard_map/ppermute | solution.py:17
  3.8 0.8 slice.163
  4.5 4.5 %collective-permute-start.2 = (bf16[2,2048]{1,0:T(2,128)(2,1)S(1)}, bf16[2,2048]{1,0:T(2,128)(2,1)S(1)}, u32[]{:S(2)}, u32[]{:S(2)}) collective-permute-start(bf16[2,2048]{1,0:T(2,128)(2,1)S(1)} %slice.163), channel_id=1, source_target_pairs={{0,4},{4,8},{8,12},{12,16},{16,20},{20,24},{24,28},{1,5},{5,9},{9,... | collective-permute-start | bytes 24584 | tf_op jit(solution)/shard_map/ppermute | solution.py:17
  9.1 1.4 %slice.149 = bf16[2,2048]{1,0:T(2,128)(2,1)} slice(bf16[128,2048]{1,0:T(8,128)(2,1)} %param.10), slice={[126:128], [0:2048]} | slice | bytes 16384 | tf_op jit(solution)/shard_map/slice | solution.py:44
  10.4 2.5 %collective-permute-start = (bf16[2,2048]{1,0:T(2,128)(2,1)}, bf16[2,2048]{1,0:T(2,128)(2,1)}, u32[]{:S(2)}, u32[]{:S(2)}) collective-permute-start(bf16[2,2048]{1,0:T(2,128)(2,1)} %slice.149), channel_id=1, source_target_pairs={{0,4},{4,8},{8,12},{12,16},{16,20},{20,24},{24,28},{1,5},{5,9},{9,... | collective-permute-start | bytes 24584 | tf_op jit(solution)/shard_map/ppermute | solution.py:17
  13.0 0.5 fusion.20
  13.5 0.5 multiply_convert_fusion
  14.0 1.6 %fusion.24 = (f32[1,1,2048]{2,1,0:T(1,128)S(1)}, f32[1,1,2048]{2,1,0:T(1,128)S(1)}, f32[1,1,2048]{2,1,0:T(1,128)S(1)}, f32[1,1,2048]{2,1,0:T(1,128)S(1)}, f32[1,...) fusion(f32[3,3,2048]{2,1,0:T(4,128)} %param.13), kind=kLoop, calls=%fused_computation.69 | loop fusion | bytes 147456 | tf_op jit(solution)/shard_map/slice | solution.py:24
  15.7 1.0 %fusion.21 = (f32[16,2048]{1,0:T(8,128)S(1)}, f32[16,2048]{1,0:T(8,128)S(1)}, f32[16,2048]{1,0:T(8,128)S(1)}, f32[16,2048]{1,0:T(8,128)S(1)}) fusion(f32[16,2048]{1,0:T(8,128)} %param.14, f32[16,2048]{1,0:T(8,128)} %param.15), kind=kLoop, calls=%fused_computation.66 | loop fusion | flops 163840 | bytes 786432 | tf_op jit(solution)/shard_map/mul | solution.py:35
  16.7 1.4 %exponential_multiply_fusion = (f32[16,16,2048]{2,1,0:T(8,128)S(1)}, f32[16,2048]{1,0:T(8,128)S(1)}, f32[16,16,2048]{2,1,0:T(8,128)S(1)}) fusion(f32[16]{0:T(128)S(1)} %get-tuple-element.25, f32[16,2048]{1,0:T(8,128)S(1)} %get-tuple-element.13, f32[16,2048]{1,0:T(8,128)S(1)} %get-tuple-element.14, f32[16]{0:T(128)S(1)} %get-tuple-element.24), kind=kLoop, calls=%fused_computation.4 | loop fusion | flops 3112960 | bytes 4587648 | tf_op jit(solution)/shard_map/mul | solution.py:85
  18.1 0.0 copy-start.4
  18.2 0.0 copy-start.5
  18.2 1.0 %fusion.17 = f32[16,16,2048]{2,1,0:T(8,128)S(1)} fusion(f32[16,2048]{1,0:T(8,128)S(1)} %get-tuple-element.7, f32[16,16]{1,0:T(8,128)S(1)} %iota_subtract_fusion), kind=kOutput, calls=%fused_computation.51 | convolution fusion | flops 100667392 | bytes 2229248 | tf_op jit(solution)/shard_map/dot_general | solution.py:61
  19.2 0.6 iota_multiply_fusion
  19.8 0.0 collective-permute-done.1
  19.8 0.0 copy-done.4
  19.8 0.1 maximum_convert_fusion.1
  20.0 0.0 collective-permute-done.2
  20.0 0.0 copy-done.5
  20.0 0.1 maximum_convert_fusion.2
  20.1 0.7 fusion.4
  20.8 5.8 %multiply_reduce_fusion.1 = (f32[8,16,2048]{2,1,0:T(8,128)S(1)}, f32[8,16,2048]{2,1,0:T(8,128)}) fusion(f32[16,16,2048]{2,1,0:T(8,128)S(1)} %get-tuple-element.10, f32[8,16,2048]{2,1,0:T(8,128)S(1)} %bitcast.23, f32[16,16,2048]{2,1,0:T(8,128)S(1)} %fusion.17), kind=kLoop, calls=%fused_computation.1 | loop fusion | flops 16252928 | bytes 7340032 | tf_op jit(solution)/shard_map/reduce_sum | solution.py:67
  26.6 0.1 slice_add_fusion.1
  26.8 0.9 %copy-done.3 = f32[16,2048]{1,0:T(8,128)S(1)} copy-done((f32[16,2048]{1,0:T(8,128)S(1)}, f32[16,2048]{1,0:T(8,128)}, u32[]{:S(2)}) %copy-start.3) | copy-done | bytes 131096
  27.7 0.7 pad_add_fusion
  28.4 0.7 fusion.22
  29.1 0.0 copy-done
  29.1 0.7 slice.197
  29.8 2.4 %pad.23 = f32[4,16,2048]{2,1,0:T(8,128)} pad(f32[2,16,2048]{2,1,0:T(8,128)} %pad_add_fusion, f32[]{:T(128)} %constant.13.clone.1), padding=1_0_1x0_0_0x0_0_0 | pad | bytes 786436 | tf_op jit(solution)/shard_map/pad | solution.py:69
  32.2 1.6 %pad_maximum_fusion.1 = f32[2,16,2048]{2,1,0:T(8,128)} fusion(f32[1,16,2048]{2,1,0:T(8,128)} %get-tuple-element.5, f32[1,16,2048]{2,1,0:T(8,128)S(1)} %get-tuple-element.4), kind=kLoop, calls=%fused_computation.44 | loop fusion | flops 65536 | bytes 524288 | tf_op jit(solution)/shard_map/concatenate | solution.py:69
  33.8 2.4 %pad.22 = f32[4,16,2048]{2,1,0:T(8,128)} pad(f32[2,16,2048]{2,1,0:T(8,128)} %pad_maximum_fusion.1, f32[]{:T(128)} %constant.13.clone.1), padding=0_1_1x0_0_0x0_0_0 | pad | bytes 786436 | tf_op jit(solution)/shard_map/pad | solution.py:69
  36.2 2.0 %fusion.13 = f32[3,16,2048]{2,1,0:T(8,128)} fusion(f32[4,16,2048]{2,1,0:T(8,128)} %pad.23, f32[4,16,2048]{2,1,0:T(8,128)} %pad.22, f32[8,16,2048]{2,1,0:T(8,128)} %copy-done, f32[16,2048]{1,0:T(8,128)S(1)} %get-tuple-element.12), kind=kLoop, calls=%fused_computation.40 | loop fusion | flops 294912 | bytes 1703936 | tf_op jit(solution)/shard_map/add | solution.py:35
  38.3 2.1 %add.100 = f32[4,16,2048]{2,1,0:T(8,128)} add(f32[4,16,2048]{2,1,0:T(8,128)} %pad.22, f32[4,16,2048]{2,1,0:T(8,128)} %pad.23) | non-fusion elementwise | flops 131072 | bytes 1572864 | tf_op jit(solution)/shard_map/add | solution.py:69
  40.4 4.2 %pad.25 = f32[8,16,2048]{2,1,0:T(8,128)} pad(f32[4,16,2048]{2,1,0:T(8,128)} %add.100, f32[]{:T(128)} %constant.13.clone.1), padding=1_0_1x0_0_0x0_0_0 | pad | bytes 1572868 | tf_op jit(solution)/shard_map/pad | solution.py:69
  44.5 4.1 %pad.62 = f32[7,16,2048]{2,1,0:T(8,128)} pad(f32[4,16,2048]{2,1,0:T(8,128)} %add.100, f32[]{:T(128)} %constant.13.clone.1), padding=0_0_1x0_0_0x0_0_0 | pad | bytes 1441796
  48.6 0.0 copy-done.8
  48.6 1.8 %pad_maximum_fusion = f32[4,16,2048]{2,1,0:T(8,128)} fusion(f32[3,16,2048]{2,1,0:T(8,128)} %fusion.13, f32[1,16,2048]{2,1,0:T(8,128)S(1)} %copy-done.8), kind=kLoop, calls=%fused_computation.37 | loop fusion | flops 131072 | bytes 1048576 | tf_op jit(solution)/shard_map/concatenate | solution.py:69
  50.5 4.1 %pad.24 = f32[8,16,2048]{2,1,0:T(8,128)} pad(f32[4,16,2048]{2,1,0:T(8,128)} %pad_maximum_fusion, f32[]{:T(128)} %constant.13.clone.1), padding=0_1_1x0_0_0x0_0_0 | pad | bytes 1572868 | tf_op jit(solution)/shard_map/pad | solution.py:69
  54.6 0.9 %add_convert_fusion = bf16[1,16,2048]{2,1,0:T(8,128)(2,1)S(1)} fusion(f32[7,16,2048]{2,1,0:T(8,128)} %pad.62), kind=kLoop, calls=%fused_computation.53 | loop fusion | flops 65536 | bytes 196608 | tf_op jit(solution)/shard_map/convert
  55.5 9.9 %all_gather.3 = bf16[8,16,2048]{2,1,0:T(8,128)(2,1)S(1)} all-gather(bf16[1,16,2048]{2,1,0:T(8,128)(2,1)S(1)} %add_convert_fusion), channel_id=1, replica_groups=mesh['seq'=8,'chan'=4] {'seq'}, dimensions={0}, use_global_device_ids=true | all-gather | bytes 589824 | tf_op jit(solution)/shard_map/all_gather | solution.py:73
  65.4 1.6 %slice_add_fusion = f32[7,16,2048]{2,1,0:T(8,128)S(1)} fusion(f32[8,16,2048]{2,1,0:T(8,128)} %pad.25, f32[8,16,2048]{2,1,0:T(8,128)} %pad.24), kind=kLoop, calls=%fused_computation.33 | loop fusion | flops 229376 | bytes 2752512 | tf_op jit(solution)/shard_map/add | solution.py:69
  67.0 0.0 copy-done.12
  67.0 0.0 copy-done.13
  67.0 0.3 select_reduce_fusion
  67.4 0.2 multiply_add_fusion
  67.6 4.2 %multiply_reduce_fusion = f32[8,16,2048]{2,1,0:T(8,128)S(1)} fusion(f32[8,16,2048]{2,1,0:T(8,128)S(1)} %multiply_add_fusion, f32[16,16,2048]{2,1,0:T(8,128)S(1)} %get-tuple-element.6), kind=kLoop, calls=%fused_computation | loop fusion | flops 8126464 | bytes 4194304 | tf_op jit(solution)/shard_map/reduce_sum | solution.py:86
  71.8 0.0 copy-start.6
  71.8 0.0 copy-start.7
  71.8 0.0 copy-start.9
  71.8 0.0 copy-start.10
  71.8 0.1 add.104
  72.0 0.0 collective-permute-done
  72.0 0.9 copy-done.6
  72.8 0.8 maximum_convert_fusion
  73.7 0.0 copy-done.7
  73.7 0.0 copy-done.9
  73.7 0.0 copy-done.10
  73.7 0.0 copy-start.11
  73.7 0.5 fusion.11
  74.3 0.0 copy-start.1
  74.3 0.2 fusion
  74.5 12.0 %psum.7 = f32[128]{0:T(128)S(1)} all-reduce(f32[128]{0:T(128)S(1)} %fusion), channel_id=1, replica_groups=mesh['seq'=8,'chan'=4] {'chan'}, use_global_device_ids=true, to_apply=%region_6.7 | all-reduce | flops 128 | bytes 1024 | tf_op jit(solution)/shard_map/psum | solution.py:91
  86.4 1.0 %fusion.2 = bf16[128,2048]{1,0:T(8,128)(2,1)} fusion(bf16[128,2048]{1,0:T(8,128)(2,1)S(1)} %fusion.11, f32[2048]{0:T(1024)S(1)} %copy-done.11, f32[128]{0:T(128)S(1)} %add_rsqrt_fusion), kind=kLoop, calls=%fused_computation.10 | loop fusion | flops 1048576 | bytes 1057280 | tf_op jit(solution)/shard_map/convert_element_type | solution.py:93
  (16 shorter events, 0.1 us)
Async XLA Ops:
  1.4 18.4 %collective-permute-start.1 = (bf16[2,2048]{1,0:T(2,128)(2,1)S(1)}, bf16[2,2048]{1,0:T(2,128)(2,1)S(1)}, u32[]{:S(2)}, u32[]{:S(2)}) collective-permute-start(bf16[2,2048]{1,0:T(2,128)(2,1)S(1)} %slice.156), channel_id=1, source_target_pairs={{0,4},{4,8},{8,12},{12,16},{16,20},{20,24},{24,28},{1,5},{5,9},{9,... | collective-permute-start | bytes 24584 | tf_op jit(solution)/shard_map/ppermute | solution.py:17
  4.5 15.4 %collective-permute-start.2 = (bf16[2,2048]{1,0:T(2,128)(2,1)S(1)}, bf16[2,2048]{1,0:T(2,128)(2,1)S(1)}, u32[]{:S(2)}, u32[]{:S(2)}) collective-permute-start(bf16[2,2048]{1,0:T(2,128)(2,1)S(1)} %slice.163), channel_id=1, source_target_pairs={{0,4},{4,8},{8,12},{12,16},{16,20},{20,24},{24,28},{1,5},{5,9},{9,... | collective-permute-start | bytes 24584 | tf_op jit(solution)/shard_map/ppermute | solution.py:17
  10.4 61.6 %collective-permute-start = (bf16[2,2048]{1,0:T(2,128)(2,1)}, bf16[2,2048]{1,0:T(2,128)(2,1)}, u32[]{:S(2)}, u32[]{:S(2)}) collective-permute-start(bf16[2,2048]{1,0:T(2,128)(2,1)} %slice.149), channel_id=1, source_target_pairs={{0,4},{4,8},{8,12},{12,16},{16,20},{20,24},{24,28},{1,5},{5,9},{9,... | collective-permute-start | bytes 24584 | tf_op jit(solution)/shard_map/ppermute | solution.py:17
  18.1 1.7 %copy-start.4 = (bf16[128,2048]{1,0:T(8,128)(2,1)S(1)}, bf16[128,2048]{1,0:T(8,128)(2,1)}, u32[]{:S(2)}) copy-start(bf16[128,2048]{1,0:T(8,128)(2,1)} %param.11) | copy-start | bytes 1572868
  18.2 1.8 %copy-start.5 = (bf16[128,2048]{1,0:T(8,128)(2,1)S(1)}, bf16[128,2048]{1,0:T(8,128)(2,1)}, u32[]{:S(2)}) copy-start(bf16[128,2048]{1,0:T(8,128)(2,1)} %param.12) | copy-start | bytes 1572868
  26.6 2.5 %copy-start = (f32[8,16,2048]{2,1,0:T(8,128)}, f32[8,16,2048]{2,1,0:T(8,128)S(1)}, u32[]{:S(2)}) copy-start(f32[8,16,2048]{2,1,0:T(8,128)S(1)} %get-tuple-element.2) | copy-start | bytes 3145732
  26.6 1.0 %copy-start.3 = (f32[16,2048]{1,0:T(8,128)S(1)}, f32[16,2048]{1,0:T(8,128)}, u32[]{:S(2)}) copy-start(f32[16,2048]{1,0:T(8,128)} %param.14) | copy-start | bytes 393220
  38.3 10.4 %copy-start.8 = (f32[1,16,2048]{2,1,0:T(8,128)S(1)}, f32[1,16,2048]{2,1,0:T(8,128)}, u32[]{:S(2)}) copy-start(f32[1,16,2048]{2,1,0:T(8,128)} %slice.197) | copy-start | bytes 393220
  54.6 12.4 %copy-start.12 = (pred[8]{0:T(512)(128)(4,1)S(1)}, pred[8]{0:T(512)(128)(4,1)}, u32[]{:S(2)}) copy-start(pred[8]{0:T(512)(128)(4,1)} %fusion.20) | copy-start | bytes 28
  54.6 12.4 %copy-start.13 = (f32[8]{0:T(128)S(1)}, f32[8]{0:T(128)}, u32[]{:S(2)}) copy-start(f32[8]{0:T(128)} %multiply_convert_fusion) | copy-start | bytes 100
  55.5 11.8 %copy-start.14 = (f32[8]{0:T(128)S(1)}, f32[8]{0:T(128)}, u32[]{:S(2)}) copy-start(f32[8]{0:T(128)} %iota_multiply_fusion) | copy-start | bytes 100
  67.6 4.2 %copy-start.2 = (f32[8,16,2048]{2,1,0:T(8,128)S(1)}, f32[8,16,2048]{2,1,0:T(8,128)}, u32[]{:S(2)}) copy-start(f32[8,16,2048]{2,1,0:T(8,128)} %get-tuple-element.3) | copy-start | bytes 3145732
  71.8 1.0 %copy-start.6 = (bf16[128,2048]{1,0:T(8,128)(2,1)S(1)}, bf16[128,2048]{1,0:T(8,128)(2,1)}, u32[]{:S(2)}) copy-start(bf16[128,2048]{1,0:T(8,128)(2,1)} %param.10) | copy-start | bytes 1572868
  71.8 1.9 %copy-start.7 = (bf16[128,2048]{1,0:T(8,128)(2,1)S(1)}, bf16[128,2048]{1,0:T(8,128)(2,1)}, u32[]{:S(2)}) copy-start(bf16[128,2048]{1,0:T(8,128)(2,1)} %param.9) | copy-start | bytes 1572868
  71.8 1.9 %copy-start.9 = (f32[1,1,2048]{2,1,0:T(1,128)S(1)}, f32[1,1,2048]{2,1,0:T(1,128)}, u32[]{:S(2)}) copy-start(f32[1,1,2048]{2,1,0:T(1,128)} %get-tuple-element.21) | copy-start | bytes 24580
  71.8 1.9 %copy-start.10 = (f32[2048]{0:T(1024)S(1)}, f32[2048]{0:T(1024)}, u32[]{:S(2)}) copy-start(f32[2048]{0:T(1024)} %param.16) | copy-start | bytes 24580
  73.7 12.7 %copy-start.11 = (f32[2048]{0:T(1024)S(1)}, f32[2048]{0:T(1024)}, u32[]{:S(2)}) copy-start(f32[2048]{0:T(1024)} %param.17) | copy-start | bytes 24580
  74.3 13.2 %copy-start.1 = (bf16[128,2048]{1,0:T(8,128)(2,1)}, bf16[128,2048]{1,0:T(8,128)(2,1)S(1)}, u32[]{:S(2)}) copy-start(bf16[128,2048]{1,0:T(8,128)(2,1)S(1)} %fusion.11) | copy-start | bytes 1572868
where the time goes:
time: 88.4 us; the launch traced here: 87.4 us
  other arithmetic  30 us (34%)
  local copies, waits for them, and re-layouts  24.3 us (27%)
  blocking collectives  21.9 us (25%)
  starting transfers between devices  9.37 us (11%)
  matrix products  1.02 us (1%)
  between operations  0.91 us (1%)
    pad x4, local copies, waits for them, and re-layouts, body(): lax.associative_scan(link_states, (step_decay, sub_states), axis=0)  13.1 us
    psum x1, blocking collectives, body(): row_squares = lax.psum(jnp.sum(widened * widened, axis=1), 'chan')  12 us
    all_gather x1, blocking collectives, body(): lax.all_gather(block_state[None].astype(jnp.bfloat16), 'seq', axis=0, til...  9.9 us
    ppermute x3, starting transfers between devices, shifted(): return lax.ppermute(block, axis, route)  9.37 us
    unnamed x31, local copies, waits for them, and re-layouts  5.93 us
    reduce_sum x1, other arithmetic, body(): sub_states = jnp.sum(blocks[:, :, None, :] * tail_decay[None], axis=1)  5.84 us
    add x3, other arithmetic, body(): lax.associative_scan(link_states, (step_decay, sub_states), axis=0)  4.36 us
    reduce_sum x1, other arithmetic, body(): across = jnp.sum(readout[None, :, :, :] * entering[:, None, :, :], axis=2)  4.17 us
  transfers between devices with their start and end apart: 3, of which 0 were waited for; matrix products, arithmetic and copies ran while one was open for 57% of the time, Pallas kernels for 0%

commit v1 on v0

v1 whole, which is shorter than its diff:
```python
import functools

import jax
import jax.numpy as jnp
from jax import lax
from jax.experimental import pallas as pl
from jax.experimental.pallas import tpu as pltpu
from jax.sharding import PartitionSpec as P

D = 8192
LANES = 128
epsilon = 1e-06
MESH = pl.DeviceIdType.MESH


def tree_sum(terms):
    while len(terms) > 1:
        paired = [terms[i] + terms[i + 1] for i in range(0, len(terms) - 1, 2)]
        if len(terms) % 2:
            paired.append(terms[-1])
        terms = paired
    return terms[0]


def kernel(
    seq_size,
    chan_size,
    residual_ref,
    query_ref,
    key_ref,
    value_ref,
    filter_ref,
    decay_ref,
    residue_ref,
    skip_ref,
    gain_ref,
    summed_ref,
    normed_ref,
    mix_ref,
    conv_ref,
    query_side_ref,
    stage_ref,
    rate_ref,
    factor_ref,
    weight_ref,
    total_ref,
    carried_ref,
    tail_out,
    tail_in,
    state_out,
    state_in,
    squares_ref,
    squares_out,
    squares_in,
    tail_sem,
    state_send,
    state_recv,
    chan_send,
    chan_recv,
):
    rows, width = residual_ref.shape
    poles = decay_ref.shape[0]
    groups = width // LANES
    halves = groups // 8
    pitch = rows + 8
    levels = seq_size.bit_length() - 1
    me = lax.axis_index("seq")
    my_chan = lax.axis_index("chan")
    after = lax.rem(me + 1, seq_size)
    previous = lax.rem(me + seq_size - 1, seq_size)
    partners = [
        me + (1 - 2 * lax.rem(lax.div(me, 1 << k), 2)) * (1 << k) for k in range(levels)
    ]
    chan_peers = [lax.rem(my_chan + j, chan_size) for j in range(1, chan_size)]

    barrier = pltpu.get_barrier_semaphore()
    for other in [after, previous] + partners:
        pl.semaphore_signal(barrier, inc=1, device_id={"seq": other}, device_id_type=MESH)
    for other in chan_peers:
        pl.semaphore_signal(barrier, inc=1, device_id={"chan": other}, device_id_type=MESH)

    inputs = (query_ref, key_ref, value_ref)
    for i in range(3):
        last = inputs[i][rows - 16 : rows, :].astype(jnp.float32)
        tail_out[2 * i : 2 * i + 2, :] = last[14:16, :]
    tail_out[6:8, :] = jnp.zeros((2, width), jnp.float32)
    pl.semaphore_wait(barrier, 2 + levels + chan_size - 1)
    tail_copy = pltpu.make_async_remote_copy(
        src_ref=tail_out,
        dst_ref=tail_in,
        send_sem=tail_sem.at[0],
        recv_sem=tail_sem.at[1],
        device_id={"seq": after},
        device_id_type=MESH,
    )
    tail_copy.start()

    def to_channels(source, target):
        for g in range(groups):
            stage_ref[g * poles : (g + 1) * poles, :] = source[:, g * LANES : (g + 1) * LANES]
        for p in range(poles):
            for h in range(halves):
                target[p, h * 8 : h * 8 + 8, :] = stage_ref[
                    pl.ds(h * 8 * poles + p, 8, stride=poles), :
                ]

    to_channels(decay_ref, rate_ref)
    to_channels(residue_ref, weight_ref)
    rate = rate_ref[...]
    factor_ref[...] = jnp.exp(-rate)
    weight_ref[...] = weight_ref[...] * jnp.sqrt(2.0 * rate)

    def feature(i, count, lanes, tail):
        block = inputs[i][0:count, lanes].astype(jnp.float32)
        once = pltpu.roll(block, 1, 0)
        twice = pltpu.roll(block, 2, 0)
        if tail is not None:
            row = lax.broadcasted_iota(jnp.int32, (count, LANES), 0)
            older = tail[2 * i : 2 * i + 1, :]
            newer = tail[2 * i + 1 : 2 * i + 2, :]
            once = jnp.where(row == 0, newer, once)
            twice = jnp.where(row == 0, older, jnp.where(row == 1, newer, twice))
        taps = filter_ref[i, :, lanes]
        return taps[0:1, :] * block + taps[1:2, :] * once + taps[2:3, :] * twice

    def lanes_of(g):
        return pl.ds(pl.multiple_of(g * LANES, LANES), LANES)

    def place_of(g, count):
        return pl.ds(pl.multiple_of(g * pitch, 8), count)

    def mix_all(g, _):
        lanes = lanes_of(g)
        mix_ref[place_of(g, rows), :] = feature(1, rows, lanes, None) * feature(
            2, rows, lanes, None
        )
        return 0

    lax.fori_loop(0, groups, mix_all, 0)
    tail_copy.wait()
    is_first = me == 0

    def mix_first(g, _):
        lanes = lanes_of(g)
        tail = jnp.where(is_first, 0.0, tail_in[:, lanes])
        product = feature(1, 16, lanes, tail) * feature(2, 16, lanes, tail)
        mix_ref[place_of(g, 8), :] = product[0:8, :]
        return 0

    lax.fori_loop(0, groups, mix_first, 0)

    def half_of(ref, h):
        return tuple(ref[p, h * 8 : h * 8 + 8, :] for p in range(poles))

    def token(h, t):
        return pl.ds(h * 8 * pitch + t, 8, stride=pitch)

    zeros = (jnp.zeros((8, LANES), jnp.float32),) * poles
    for h in range(halves):
        factor = half_of(factor_ref, h)

        def advance(t, state, h=h, factor=factor):
            current = mix_ref[token(h, t), :]
            return tuple(a * s + current for a, s in zip(factor, state))

        state = lax.fori_loop(0, rows, advance, zeros, unroll=8)
        for p in range(poles):
            total_ref[p, h * 8 : h * 8 + 8, :] = state[p]

    def state_copy(k):
        return pltpu.make_async_remote_copy(
            src_ref=state_out.at[k],
            dst_ref=state_in.at[k],
            send_sem=state_send.at[k],
            recv_sem=state_recv.at[k],
            device_id={"seq": partners[k]},
            device_id_type=MESH,
        )

    def query_all(g, _):
        lanes = lanes_of(g)
        tail = jnp.where(is_first, 0.0, tail_in[:, lanes])
        query_side_ref[:, lanes] = feature(0, rows, lanes, tail)
        return 0

    def local_half(h):
        factor = half_of(factor_ref, h)

        def advance(t, state):
            current = mix_ref[token(h, t), :]
            state = tuple(a * s + current for a, s in zip(factor, state))
            conv_ref[token(h, t), :] = tree_sum(
                [weight_ref[p, h * 8 : h * 8 + 8, :] * state[p] for p in range(poles)]
            )
            return state

        lax.fori_loop(0, rows, advance, zeros, unroll=8)

    beside = {0: [lambda: lax.fori_loop(0, groups, query_all, 0)]}
    for h in range(halves):
        beside.setdefault(min(1 + h, levels - 1), []).append(functools.partial(local_half, h))
    carried_ref[...] = jnp.zeros_like(carried_ref)
    for k in range(levels):
        state_out[k] = total_ref[...].astype(jnp.bfloat16)
        copy = state_copy(k)
        copy.start()
        for work in beside.get(k, []):
            work()
        copy.wait()
        size = 1 << k
        inside = lax.rem(me, size)
        upper = lax.rem(lax.div(me, size), 2) == 1
        span = (rows * inside).astype(jnp.float32)
        rate = rate_ref[...]
        arrived = state_in[k].astype(jnp.float32)
        carried_ref[...] += jnp.where(upper, jnp.exp(-rate * span) * arrived, 0.0)
        if k < levels - 1:
            own = total_ref[...]
            early = jnp.where(upper, arrived, own)
            late = jnp.where(upper, own, arrived)
            total_ref[...] = late + jnp.exp(-rate * (rows * size)) * early

    for h in range(halves):
        factor = half_of(factor_ref, h)
        start = tuple(
            weight_ref[p, h * 8 : h * 8 + 8, :] * carried_ref[p, h * 8 : h * 8 + 8, :]
            for p in range(poles)
        )

        def across(t, state, h=h, factor=factor):
            state = tuple(a * s for a, s in zip(factor, state))
            conv_ref[token(h, t), :] = conv_ref[token(h, t), :] + tree_sum(list(state))
            return state

        lax.fori_loop(0, rows, across, start, unroll=8)

    padded = squares_ref.shape[0]
    squares_ref[...] = jnp.zeros_like(squares_ref)

    def gate(g, _):
        lanes = lanes_of(g)
        place = place_of(g, rows)
        gated = query_side_ref[:, lanes] * (
            conv_ref[place, :] + skip_ref[:, lanes] * mix_ref[place, :]
        )
        summed = (residual_ref[:, lanes].astype(jnp.float32) + gated).astype(jnp.bfloat16)
        summed_ref[:, lanes] = summed
        widened = summed.astype(jnp.float32)
        squares_ref[0:rows, :] += widened * widened
        return 0

    lax.fori_loop(0, groups, gate, 0)
    row_squares = jnp.sum(jnp.transpose(squares_ref[...]), axis=0, keepdims=True)
    squares_out[...] = jnp.broadcast_to(row_squares, (8, padded))
    chan_copies = [
        pltpu.make_async_remote_copy(
            src_ref=squares_out,
            dst_ref=squares_in.at[j],
            send_sem=chan_send.at[j],
            recv_sem=chan_recv.at[j],
            device_id={"chan": chan_peers[j]},
            device_id_type=MESH,
        )
        for j in range(chan_size - 1)
    ]
    for copy in chan_copies:
        copy.start()
    for copy in chan_copies:
        copy.wait()
    together = squares_out[...]
    for j in range(chan_size - 1):
        together = together + squares_in[j]
    inverse = lax.rsqrt(together * (1.0 / D) + epsilon)
    squares_ref[...] = jnp.transpose(jnp.broadcast_to(inverse[0:1, :], (LANES, padded)))

    def normalize(g, _):
        lanes = lanes_of(g)
        widened = summed_ref[:, lanes].astype(jnp.float32)
        normed_ref[:, lanes] = (
            widened * squares_ref[0:rows, :] * gain_ref[:, lanes]
        ).astype(jnp.bfloat16)
        return 0

    lax.fori_loop(0, groups, normalize, 0)


def body(
    seq_size,
    chan_size,
    residual,
    query_in,
    key_in,
    value_in,
    short_filter,
    decay_rate,
    residue,
    skip_gain,
    norm_gain,
):
    rows, width = residual.shape
    poles = decay_rate.shape[0]
    groups = width // LANES
    levels = seq_size.bit_length() - 1
    padded = -(-rows // LANES) * LANES
    vmem = pl.BlockSpec(memory_space=pltpu.VMEM)
    f32, bf16 = jnp.float32, jnp.bfloat16
    by_channel = (poles, groups, LANES)
    return pl.pallas_call(
        functools.partial(kernel, seq_size, chan_size),
        out_shape=(jax.ShapeDtypeStruct((rows, width), bf16),) * 2,
        in_specs=[vmem] * 9,
        out_specs=(vmem, vmem),
        scratch_shapes=[
            pltpu.VMEM((groups * (rows + 8), LANES), f32),
            pltpu.VMEM((groups * (rows + 8), LANES), f32),
            pltpu.VMEM((rows, width), f32),
            pltpu.VMEM((groups * poles, LANES), f32),
            pltpu.VMEM(by_channel, f32),
            pltpu.VMEM(by_channel, f32),
            pltpu.VMEM(by_channel, f32),
            pltpu.VMEM(by_channel, f32),
            pltpu.VMEM(by_channel, f32),
            pltpu.VMEM((8, width), f32),
            pltpu.VMEM((8, width), f32),
            pltpu.VMEM((levels,) + by_channel, bf16),
            pltpu.VMEM((levels,) + by_channel, bf16),
            pltpu.VMEM((padded, LANES), f32),
            pltpu.VMEM((8, padded), f32),
            pltpu.VMEM((chan_size - 1, 8, padded), f32),
            pltpu.SemaphoreType.DMA((2,)),
            pltpu.SemaphoreType.DMA((levels,)),
            pltpu.SemaphoreType.DMA((levels,)),
            pltpu.SemaphoreType.DMA((chan_size - 1,)),
            pltpu.SemaphoreType.DMA((chan_size - 1,)),
        ],
        compiler_params=pltpu.CompilerParams(
            collective_id=0, has_side_effects=True, vmem_limit_bytes=40 * 1024 * 1024
        ),
    )(
        residual,
        query_in,
        key_in,
        value_in,
        short_filter,
        decay_rate,
        residue,
        skip_gain[None],
        norm_gain[None],
    )


def solution(mesh):
    in_specs = (
        P("seq", "chan"),
        P("seq", "chan"),
        P("seq", "chan"),
        P("seq", "chan"),
        P(None, None, "chan"),
        P(None, "chan"),
        P(None, "chan"),
        P("chan"),
        P("chan"),
    )
    out_specs = (P("seq", "chan"), P("seq", "chan"))
    return jax.shard_map(
        functools.partial(body, mesh.shape["seq"], mesh.shape["chan"]),
        mesh=mesh,
        in_specs=in_specs,
        out_specs=out_specs,
        check_vma=False,
    )
```

time: 88.4 us -> 34.3 us (0.39)
  other arithmetic: 30 us -> 0 us
  Pallas kernels: 0 us -> 23.4 us
  blocking collectives: 21.9 us -> 0 us
  local copies, waits for them, and re-layouts: 24.3 us -> 9.84 us
  starting transfers between devices: 9.37 us -> 0 us
  matrix products: 1.02 us -> 0 us
    pallas_call x0 -> x1, Pallas kernels: none -> 23.4 us  [body(): pl.pallas_call(functools.partial(kernel, seq_size, chan_size), out_shape=...]
    pad x4 -> x0, local copies, waits for them, and re-layouts: 13.1 us -> none  [body(): lax.associative_scan(link_states, (step_decay, sub_states), axis=0)]
    psum x1 -> x0, blocking collectives: 12 us -> none  [body(): row_squares = lax.psum(jnp.sum(widened * widened, axis=1), 'chan')]
    reduce_sum x4 -> x0, other arithmetic: 10.5 us -> none  [the longest x1 5.84 us: body(): sub_states = jnp.sum(blocks[:, :, None, :] * tail_decay[None], axis=1)]
    all_gather x1 -> x0, blocking collectives: 9.9 us -> none  [body(): lax.all_gather(block_state[None].astype(jnp.bfloat16), 'seq', axis=0, til...]
    ppermute x3 -> x0, starting transfers between devices: 9.37 us -> none  [shifted(): return lax.ppermute(block, axis, route)]
    add x8 -> x0, other arithmetic: 6.87 us -> none  [the longest x3 4.36 us: body(): lax.associative_scan(link_states, (step_decay, sub_states), axis=0)]
    slice x5 -> x0, local copies, waits for them, and re-layouts: 5.21 us -> none  [the longest x1 1.65 us: short_features(): result = tap_weights[0][None, :] * extended[lag_rows:lag_rows + token_rows]]
  transfers between devices with their start and end apart: 3 -> 0, of which waited for: 0 -> 0; matrix products, arithmetic and copies ran while one was open for 57% -> 0% of each run, Pallas kernels for 0% -> 0%
where the time goes in v1:
time: 34.3 us; the launch traced here: 33.9 us
  Pallas kernels  23.4 us (68%)
  local copies, waits for them, and re-layouts  9.84 us (29%)
  between operations  0.66 us (2%)
    pallas_call x1, Pallas kernels, body(): pl.pallas_call(functools.partial(kernel, seq_size, chan_size), out_shape=...  23.4 us
    unnamed x20, local copies, waits for them, and re-layouts  9.84 us

profile of v1, /device:TPU:0, one launch (start us, length us, event | category | flops | bytes accessed | tf_op | source)
XLA Modules:
  0.0 33.9 jit_solution(18068911987368353464)
XLA Ops:
  0.6 0.0 copy-start
  0.6 1.0 %copy-done = bf16[128,2048]{1,0:T(8,128)(2,1)S(1)} copy-done((bf16[128,2048]{1,0:T(8,128)(2,1)S(1)}, bf16[128,2048]{1,0:T(8,128)(2,1)}, u32[]{:S(2)}) %copy-start) | copy-done | bytes 524312
  1.7 0.0 copy-start.1
  1.7 1.0 %copy-done.1 = bf16[128,2048]{1,0:T(8,128)(2,1)S(1)} copy-done((bf16[128,2048]{1,0:T(8,128)(2,1)S(1)}, bf16[128,2048]{1,0:T(8,128)(2,1)}, u32[]{:S(2)}) %copy-start.1) | copy-done | bytes 524312
  2.7 0.0 copy-start.2
  2.7 1.0 %copy-done.2 = bf16[128,2048]{1,0:T(8,128)(2,1)S(1)} copy-done((bf16[128,2048]{1,0:T(8,128)(2,1)S(1)}, bf16[128,2048]{1,0:T(8,128)(2,1)}, u32[]{:S(2)}) %copy-start.2) | copy-done | bytes 524312
  3.8 0.0 copy-start.3
  3.8 1.0 %copy-done.3 = bf16[128,2048]{1,0:T(8,128)(2,1)S(1)} copy-done((bf16[128,2048]{1,0:T(8,128)(2,1)S(1)}, bf16[128,2048]{1,0:T(8,128)(2,1)}, u32[]{:S(2)}) %copy-start.3) | copy-done | bytes 524312
  4.8 0.0 copy-start.4
  4.8 0.9 %copy-done.4 = f32[16,2048]{1,0:T(8,128)S(1)} copy-done((f32[16,2048]{1,0:T(8,128)S(1)}, f32[16,2048]{1,0:T(8,128)}, u32[]{:S(2)}) %copy-start.4) | copy-done | bytes 131096
  5.7 0.0 copy-start.5
  5.7 0.9 %copy-done.5 = f32[16,2048]{1,0:T(8,128)S(1)} copy-done((f32[16,2048]{1,0:T(8,128)S(1)}, f32[16,2048]{1,0:T(8,128)}, u32[]{:S(2)}) %copy-start.5) | copy-done | bytes 131096
  6.6 0.0 copy-start.6
  6.6 0.9 %copy-done.6 = f32[3,3,2048]{2,1,0:T(4,128)S(1)} copy-done((f32[3,3,2048]{2,1,0:T(4,128)S(1)}, f32[3,3,2048]{2,1,0:T(4,128)}, u32[]{:S(2)}) %copy-start.6) | copy-done | bytes 73752
  7.5 0.0 copy-start.7
  7.5 0.7 %copy-done.7 = f32[2048]{0:T(1024)S(1)} copy-done((f32[2048]{0:T(1024)S(1)}, f32[2048]{0:T(1024)}, u32[]{:S(2)}) %copy-start.7) | copy-done | bytes 8216
  8.2 0.0 copy-start.8
  8.2 0.7 %copy-done.8 = f32[2048]{0:T(1024)S(1)} copy-done((f32[2048]{0:T(1024)S(1)}, f32[2048]{0:T(1024)}, u32[]{:S(2)}) %copy-start.8) | copy-done | bytes 8216
  8.9 23.4 %shard_map.104 = (bf16[128,2048]{1,0:T(8,128)(2,1)S(1)}, bf16[128,2048]{1,0:T(8,128)(2,1)S(1)}) custom-call(bf16[128,2048]{1,0:T(8,128)(2,1)S(1)} %copy-done, bf16[128,2048]{1,0:T(8,128)(2,1)S(1)} %copy-done.1, bf16[128,2048]{1,0:T(8,128)(2,1)S(1)} %copy-done.2, bf16[128,2048]{1,0:T(8,128)(2,1)S(1)} %copy-done.3, f32[3,3,2048]{2,1,0:T(4,128)S(1)} %copy-done.6, ...), custom_call_target="tpu_custom_call" | custom-call | tf_op jit(solution)/shard_map/pallas_call | solution.py:308
  32.3 0.8 %copy.13 = bf16[128,2048]{1,0:T(8,128)(2,1)} copy(bf16[128,2048]{1,0:T(8,128)(2,1)S(1)} %get-tuple-element.4) | data formatting | bytes 1048576
  33.1 0.8 %copy.14 = bf16[128,2048]{1,0:T(8,128)(2,1)} copy(bf16[128,2048]{1,0:T(8,128)(2,1)S(1)} %get-tuple-element.5) | data formatting | bytes 1048576
Async XLA Ops:
  0.6 1.0 %copy-start = (bf16[128,2048]{1,0:T(8,128)(2,1)S(1)}, bf16[128,2048]{1,0:T(8,128)(2,1)}, u32[]{:S(2)}) copy-start(bf16[128,2048]{1,0:T(8,128)(2,1)} %residual_ref.1) | copy-start | bytes 1572868
  1.7 1.0 %copy-start.1 = (bf16[128,2048]{1,0:T(8,128)(2,1)S(1)}, bf16[128,2048]{1,0:T(8,128)(2,1)}, u32[]{:S(2)}) copy-start(bf16[128,2048]{1,0:T(8,128)(2,1)} %query_ref.1) | copy-start | bytes 1572868
  2.7 1.0 %copy-start.2 = (bf16[128,2048]{1,0:T(8,128)(2,1)S(1)}, bf16[128,2048]{1,0:T(8,128)(2,1)}, u32[]{:S(2)}) copy-start(bf16[128,2048]{1,0:T(8,128)(2,1)} %key_ref.1) | copy-start | bytes 1572868
  3.8 1.0 %copy-start.3 = (bf16[128,2048]{1,0:T(8,128)(2,1)S(1)}, bf16[128,2048]{1,0:T(8,128)(2,1)}, u32[]{:S(2)}) copy-start(bf16[128,2048]{1,0:T(8,128)(2,1)} %value_ref.1) | copy-start | bytes 1572868
  4.8 0.9 %copy-start.4 = (f32[16,2048]{1,0:T(8,128)S(1)}, f32[16,2048]{1,0:T(8,128)}, u32[]{:S(2)}) copy-start(f32[16,2048]{1,0:T(8,128)} %decay_ref.1) | copy-start | bytes 393220
  5.7 0.9 %copy-start.5 = (f32[16,2048]{1,0:T(8,128)S(1)}, f32[16,2048]{1,0:T(8,128)}, u32[]{:S(2)}) copy-start(f32[16,2048]{1,0:T(8,128)} %residue_ref.1) | copy-start | bytes 393220
  6.6 0.9 %copy-start.6 = (f32[3,3,2048]{2,1,0:T(4,128)S(1)}, f32[3,3,2048]{2,1,0:T(4,128)}, u32[]{:S(2)}) copy-start(f32[3,3,2048]{2,1,0:T(4,128)} %filter_ref.1) | copy-start | bytes 221188
  7.5 0.7 %copy-start.7 = (f32[2048]{0:T(1024)S(1)}, f32[2048]{0:T(1024)}, u32[]{:S(2)}) copy-start(f32[2048]{0:T(1024)} %param.16) | copy-start | bytes 24580
  8.2 0.7 %copy-start.8 = (f32[2048]{0:T(1024)S(1)}, f32[2048]{0:T(1024)}, u32[]{:S(2)}) copy-start(f32[2048]{0:T(1024)} %param.17) | copy-start | bytes 24580

commit v2 on v1

--- a/solution.py
+++ b/solution.py
@@ -25,6 +25,19 @@
 def kernel(
     seq_size,
     chan_size,
+    residual_hbm,
+    query_hbm,
+    key_hbm,
+    value_hbm,
+    filter_hbm,
+    decay_hbm,
+    residue_hbm,
+    skip_hbm,
+    summed_hbm,
+    inverse_hbm,
+    summed_ref,
+    inverse_ref,
+    store_sem,
     residual_ref,
     query_ref,
     key_ref,
@@ -33,9 +46,8 @@
     decay_ref,
     residue_ref,
     skip_ref,
-    gain_ref,
-    summed_ref,
-    normed_ref,
+    ends_ref,
+    load_sem,
     mix_ref,
     conv_ref,
     query_side_ref,
@@ -80,8 +92,27 @@
         pl.semaphore_signal(barrier, inc=1, device_id={"chan": other}, device_id_type=MESH)
 
     inputs = (query_ref, key_ref, value_ref)
+    sources = (query_hbm, key_hbm, value_hbm)
+    pairs = [(sources[i].at[rows - 16 : rows, :], ends_ref.at[i]) for i in range(3)] + [
+        (decay_hbm, decay_ref),
+        (residue_hbm, residue_ref),
+        (filter_hbm, filter_ref),
+        (key_hbm, key_ref),
+        (value_hbm, value_ref),
+        (query_hbm, query_ref),
+        (residual_hbm, residual_ref),
+        (skip_hbm, skip_ref),
+    ]
+    loads = [
+        pltpu.make_async_copy(source, target, load_sem.at[i])
+        for i, (source, target) in enumerate(pairs)
+    ]
+    for load in loads:
+        load.start()
+    for load in loads[:3]:
+        load.wait()
     for i in range(3):
-        last = inputs[i][rows - 16 : rows, :].astype(jnp.float32)
+        last = ends_ref[i].astype(jnp.float32)
         tail_out[2 * i : 2 * i + 2, :] = last[14:16, :]
     tail_out[6:8, :] = jnp.zeros((2, width), jnp.float32)
     pl.semaphore_wait(barrier, 2 + levels + chan_size - 1)
@@ -104,6 +135,8 @@
                     pl.ds(h * 8 * poles + p, 8, stride=poles), :
                 ]
 
+    for load in loads[3:5]:
+        load.wait()
     to_channels(decay_ref, rate_ref)
     to_channels(residue_ref, weight_ref)
     rate = rate_ref[...]
@@ -136,6 +169,8 @@
         )
         return 0
 
+    for load in loads[5:8]:
+        load.wait()
     lax.fori_loop(0, groups, mix_all, 0)
     tail_copy.wait()
     is_first = me == 0
@@ -196,7 +231,12 @@
 
         lax.fori_loop(0, rows, advance, zeros, unroll=8)
 
-    beside = {0: [lambda: lax.fori_loop(0, groups, query_all, 0)]}
+    def query_work():
+        for load in loads[8:]:
+            load.wait()
+        lax.fori_loop(0, groups, query_all, 0)
+
+    beside = {0: [query_work]}
     for h in range(halves):
         beside.setdefault(min(1 + h, levels - 1), []).append(functools.partial(local_half, h))
     carried_ref[...] = jnp.zeros_like(carried_ref)
@@ -250,6 +290,8 @@
         return 0
 
     lax.fori_loop(0, groups, gate, 0)
+    store_summed = pltpu.make_async_copy(summed_ref, summed_hbm, store_sem.at[0])
+    store_summed.start()
     row_squares = jnp.sum(jnp.transpose(squares_ref[...]), axis=0, keepdims=True)
     squares_out[...] = jnp.broadcast_to(row_squares, (8, padded))
     chan_copies = [
@@ -271,17 +313,64 @@
     for j in range(chan_size - 1):
         together = together + squares_in[j]
     inverse = lax.rsqrt(together * (1.0 / D) + epsilon)
-    squares_ref[...] = jnp.transpose(jnp.broadcast_to(inverse[0:1, :], (LANES, padded)))
-
-    def normalize(g, _):
-        lanes = lanes_of(g)
-        widened = summed_ref[:, lanes].astype(jnp.float32)
-        normed_ref[:, lanes] = (
-            widened * squares_ref[0:rows, :] * gain_ref[:, lanes]
-        ).astype(jnp.bfloat16)
-        return 0
-
-    lax.fori_loop(0, groups, normalize, 0)
+    inverse_ref[...] = jnp.transpose(jnp.broadcast_to(inverse[0:1, :], (LANES, padded)))[
+        0:rows, :
+    ]
+    store_inverse = pltpu.make_async_copy(inverse_ref, inverse_hbm, store_sem.at[1])
+    store_inverse.start()
+    store_summed.wait()
+    store_inverse.wait()
+
+
+def finish(
+    summed_hbm,
+    inverse_hbm,
+    gain_hbm,
+    summed_out,
+    normed_out,
+    summed_ref,
+    inverse_ref,
+    gain_ref,
+    normed_ref,
+    load_sem,
+    piece_in,
+    summed_sem,
+    normed_sem,
+):
+    pieces, each, width = normed_ref.shape
+    spans = [slice(piece * each, (piece + 1) * each) for piece in range(pieces)]
+    loads = [
+        pltpu.make_async_copy(inverse_hbm, inverse_ref, load_sem.at[0]),
+        pltpu.make_async_copy(gain_hbm, gain_ref, load_sem.at[1]),
+    ]
+    arrivals = [
+        pltpu.make_async_copy(summed_hbm.at[spans[i], :], summed_ref.at[i], piece_in.at[i])
+        for i in range(pieces)
+    ]
+    for load in loads + arrivals:
+        load.start()
+    for load in loads:
+        load.wait()
+    stores = []
+    for i in range(pieces):
+        arrivals[i].wait()
+        keep = pltpu.make_async_copy(
+            summed_ref.at[i], summed_out.at[spans[i], :], summed_sem.at[i]
+        )
+        keep.start()
+        for g in range(width // LANES):
+            lanes = slice(g * LANES, (g + 1) * LANES)
+            widened = summed_ref[i, :, lanes].astype(jnp.float32)
+            normed_ref[i, :, lanes] = (
+                widened * inverse_ref[spans[i], :] * gain_ref[:, lanes]
+            ).astype(jnp.bfloat16)
+        store = pltpu.make_async_copy(
+            normed_ref.at[i], normed_out.at[spans[i], :], normed_sem.at[i]
+        )
+        store.start()
+        stores += [keep, store]
+    for store in stores:
+        store.wait()
 
 
 def body(
@@ -302,15 +391,32 @@
     groups = width // LANES
     levels = seq_size.bit_length() - 1
     padded = -(-rows // LANES) * LANES
-    vmem = pl.BlockSpec(memory_space=pltpu.VMEM)
     f32, bf16 = jnp.float32, jnp.bfloat16
     by_channel = (poles, groups, LANES)
-    return pl.pallas_call(
+    hbm = pl.BlockSpec(memory_space=pltpu.HBM)
+    whole = jax.ShapeDtypeStruct((rows, width), bf16)
+    summed, inverse = pl.pallas_call(
         functools.partial(kernel, seq_size, chan_size),
-        out_shape=(jax.ShapeDtypeStruct((rows, width), bf16),) * 2,
-        in_specs=[vmem] * 9,
-        out_specs=(vmem, vmem),
+        out_shape=(
+            whole,
+            jax.ShapeDtypeStruct((rows, LANES), f32),
+        ),
+        in_specs=[hbm] * 8,
+        out_specs=(hbm, hbm),
         scratch_shapes=[
+            pltpu.VMEM((rows, width), bf16),
+            pltpu.VMEM((rows, LANES), f32),
+            pltpu.SemaphoreType.DMA((2,)),
+            pltpu.VMEM((rows, width), bf16),
+            pltpu.VMEM((rows, width), bf16),
+            pltpu.VMEM((rows, width), bf16),
+            pltpu.VMEM((rows, width), bf16),
+            pltpu.VMEM(short_filter.shape, f32),
+            pltpu.VMEM((poles, width), f32),
+            pltpu.VMEM((poles, width), f32),
+            pltpu.VMEM((1, width), f32),
+            pltpu.VMEM((3, 16, width), bf16),
+            pltpu.SemaphoreType.DMA((11,)),
             pltpu.VMEM((groups * (rows + 8), LANES), f32),
             pltpu.VMEM((groups * (rows + 8), LANES), f32),
             pltpu.VMEM((rows, width), f32),
@@ -334,7 +440,7 @@
             pltpu.SemaphoreType.DMA((chan_size - 1,)),
         ],
         compiler_params=pltpu.CompilerParams(
-            collective_id=0, has_side_effects=True, vmem_limit_bytes=40 * 1024 * 1024
+            collective_id=0, has_side_effects=True, vmem_limit_bytes=58 * 1024 * 1024
         ),
     )(
         residual,
@@ -345,8 +451,25 @@
         decay_rate,
         residue,
         skip_gain[None],
-        norm_gain[None],
     )
+    pieces = rows // 32
+    return pl.pallas_call(
+        finish,
+        out_shape=(whole, whole),
+        in_specs=[hbm] * 3,
+        out_specs=(hbm, hbm),
+        scratch_shapes=[
+            pltpu.VMEM((pieces, 32, width), bf16),
+            pltpu.VMEM((rows, LANES), f32),
+            pltpu.VMEM((1, width), f32),
+            pltpu.VMEM((pieces, 32, width), bf16),
+            pltpu.SemaphoreType.DMA((2,)),
+            pltpu.SemaphoreType.DMA((pieces,)),
+            pltpu.SemaphoreType.DMA((pieces,)),
+            pltpu.SemaphoreType.DMA((pieces,)),
+        ],
+        compiler_params=pltpu.CompilerParams(vmem_limit_bytes=58 * 1024 * 1024),
+    )(summed, inverse, norm_gain[None])
 
 
 def solution(mesh):

time: 34.3 us -> 26.7 us (0.78)
  local copies, waits for them, and re-layouts: 9.84 us -> 0 us
  Pallas kernels: 23.4 us -> 25.9 us
    unnamed x20 -> x0, local copies, waits for them, and re-layouts: 9.84 us -> none
    pallas_call x0 -> x1, Pallas kernels: none -> 2.05 us  [body(): pl.pallas_call(finish, out_shape=(whole, whole), in_specs=[hbm] * 3, out_...]
    pallas_call x1, Pallas kernels: 23.4 us -> 23.9 us  [body(): pl.pallas_call(functools.partial(kernel, seq_size, chan_size), out_shape=...]
where the time goes in v2:
time: 26.7 us; the launch traced here: 26.6 us
  Pallas kernels  25.9 us (97%)
  between operations  0.64 us (2%)
    pallas_call x1, Pallas kernels, body(): pl.pallas_call(functools.partial(kernel, seq_size, chan_size), out_shape=...  23.9 us
    pallas_call x1, Pallas kernels, body(): pl.pallas_call(finish, out_shape=(whole, whole), in_specs=[hbm] * 3, out_...  2.05 us

profile of v2, /device:TPU:0, one launch (start us, length us, event | category | flops | bytes accessed | tf_op | source)
XLA Modules:
  0.0 26.6 jit_solution(12078574563968372240)
XLA Ops:
  0.6 23.9 %shard_map.104 = (bf16[128,2048]{1,0:T(8,128)(2,1)}, f32[128,128]{1,0:T(8,128)}) custom-call(bf16[128,2048]{1,0:T(8,128)(2,1)} %residual_hbm.1, bf16[128,2048]{1,0:T(8,128)(2,1)} %query_hbm.1, bf16[128,2048]{1,0:T(8,128)(2,1)} %key_hbm.1, bf16[128,2048]{1,0:T(8,128)(2,1)} %value_hbm.1, f32[3,3,2048]{2,1,0:T(4,128)} %filter_hbm.1, f32[16,2048]{1,0:T(8,128)} %decay_hbm.1, ...), custom_call_target="tpu_custom_call" | custom-call | tf_op jit(solution)/shard_map/pallas_call | solution.py:398
  24.5 2.0 %shard_map.105 = (bf16[128,2048]{1,0:T(8,128)(2,1)}, bf16[128,2048]{1,0:T(8,128)(2,1)}) custom-call(bf16[128,2048]{1,0:T(8,128)(2,1)} %get-tuple-element.4.summed_hbm, f32[128,128]{1,0:T(8,128)} %get-tuple-element.5.inverse_hbm, f32[1,2048]{1,0:T(1,128)} %bitcast.3), custom_call_target="tpu_custom_call" | custom-call | tf_op jit(solution)/shard_map/pallas_call | solution.py:456

commit v3 on v2

--- a/solution.py
+++ b/solution.py
@@ -20,6 +20,15 @@
             paired.append(terms[-1])
         terms = paired
     return terms[0]
+
+
+def radices_of(seq_size):
+    radices = [2]
+    rest = seq_size // 2
+    while rest > 1:
+        radices.append(4 if rest % 4 == 0 else 2)
+        rest //= radices[-1]
+    return radices
 
 
 def kernel(
@@ -75,18 +84,27 @@
     groups = width // LANES
     halves = groups // 8
     pitch = rows + 8
-    levels = seq_size.bit_length() - 1
+    radices = radices_of(seq_size)
+    levels = len(radices)
     me = lax.axis_index("seq")
     my_chan = lax.axis_index("chan")
     after = lax.rem(me + 1, seq_size)
     previous = lax.rem(me + seq_size - 1, seq_size)
-    partners = [
-        me + (1 - 2 * lax.rem(lax.div(me, 1 << k), 2)) * (1 << k) for k in range(levels)
-    ]
+    sizes, digits, partners = [], [], []
+    size = 1
+    for radix in radices:
+        digit = lax.rem(lax.div(me, size), radix)
+        sizes.append(size)
+        digits.append(digit)
+        partners.append(
+            [me + (lax.rem(digit + j, radix) - digit) * size for j in range(1, radix)]
+        )
+        size *= radix
+    every_partner = [other for level in partners for other in level]
     chan_peers = [lax.rem(my_chan + j, chan_size) for j in range(1, chan_size)]
 
     barrier = pltpu.get_barrier_semaphore()
-    for other in [after, previous] + partners:
+    for other in [after, previous] + every_partner:
         pl.semaphore_signal(barrier, inc=1, device_id={"seq": other}, device_id_type=MESH)
     for other in chan_peers:
         pl.semaphore_signal(barrier, inc=1, device_id={"chan": other}, device_id_type=MESH)
@@ -109,23 +127,6 @@
     ]
     for load in loads:
         load.start()
-    for load in loads[:3]:
-        load.wait()
-    for i in range(3):
-        last = ends_ref[i].astype(jnp.float32)
-        tail_out[2 * i : 2 * i + 2, :] = last[14:16, :]
-    tail_out[6:8, :] = jnp.zeros((2, width), jnp.float32)
-    pl.semaphore_wait(barrier, 2 + levels + chan_size - 1)
-    tail_copy = pltpu.make_async_remote_copy(
-        src_ref=tail_out,
-        dst_ref=tail_in,
-        send_sem=tail_sem.at[0],
-        recv_sem=tail_sem.at[1],
-        device_id={"seq": after},
-        device_id_type=MESH,
-    )
-    tail_copy.start()
-
     def to_channels(source, target):
         for g in range(groups):
             stage_ref[g * poles : (g + 1) * poles, :] = source[:, g * LANES : (g + 1) * LANES]
@@ -167,11 +168,50 @@
         mix_ref[place_of(g, rows), :] = feature(1, rows, lanes, None) * feature(
             2, rows, lanes, None
         )
+        mix_ref[place_of(g, 2), :] = jnp.zeros((2, LANES), jnp.float32)
         return 0
 
     for load in loads[5:8]:
         load.wait()
     lax.fori_loop(0, groups, mix_all, 0)
+    for load in loads[:3]:
+        load.wait()
+    for i in range(3):
+        last = ends_ref[i].astype(jnp.float32)
+        tail_out[2 * i : 2 * i + 2, :] = last[14:16, :]
+    tail_out[6:8, :] = jnp.zeros((2, width), jnp.float32)
+    pl.semaphore_wait(barrier, 2 + len(every_partner) + chan_size - 1)
+    tail_copy = pltpu.make_async_remote_copy(
+        src_ref=tail_out,
+        dst_ref=tail_in,
+        send_sem=tail_sem.at[0],
+        recv_sem=tail_sem.at[1],
+        device_id={"seq": after},
+        device_id_type=MESH,
+    )
+    tail_copy.start()
+
+    def half_of(ref, h):
+        return tuple(ref[p, h * 8 : h * 8 + 8, :] for p in range(poles))
+
+    def token(h, t):
+        return pl.ds(h * 8 * pitch + t, 8, stride=pitch)
+
+    def first_tokens(t):
+        return jnp.concatenate([mix_ref[token(h, t), :] for h in range(halves)], axis=0)[None]
+
+    zeros = (jnp.zeros((8, LANES), jnp.float32),) * poles
+    for h in range(halves):
+        factor = half_of(factor_ref, h)
+
+        def advance(t, state, h=h, factor=factor):
+            current = mix_ref[token(h, t), :]
+            return tuple(a * s + current for a, s in zip(factor, state))
+
+        state = lax.fori_loop(0, rows, advance, zeros, unroll=8)
+        for p in range(poles):
+            total_ref[p, h * 8 : h * 8 + 8, :] = state[p]
+
     tail_copy.wait()
     is_first = me == 0
 
@@ -184,31 +224,21 @@
 
     lax.fori_loop(0, groups, mix_first, 0)
 
-    def half_of(ref, h):
-        return tuple(ref[p, h * 8 : h * 8 + 8, :] for p in range(poles))
-
-    def token(h, t):
-        return pl.ds(h * 8 * pitch + t, 8, stride=pitch)
-
-    zeros = (jnp.zeros((8, LANES), jnp.float32),) * poles
-    for h in range(halves):
-        factor = half_of(factor_ref, h)
-
-        def advance(t, state, h=h, factor=factor):
-            current = mix_ref[token(h, t), :]
-            return tuple(a * s + current for a, s in zip(factor, state))
-
-        state = lax.fori_loop(0, rows, advance, zeros, unroll=8)
-        for p in range(poles):
-            total_ref[p, h * 8 : h * 8 + 8, :] = state[p]
-
-    def state_copy(k):
+    reach = jnp.exp(-rate_ref[...] * (rows - 2.0))
+    total_ref[...] = total_ref[...] + reach * (factor_ref[...] * first_tokens(0) + first_tokens(1))
+
+    slots = {}
+    for k in range(levels):
+        for j in range(1, radices[k]):
+            slots[k, j] = len(slots)
+
+    def state_copy(k, j):
         return pltpu.make_async_remote_copy(
             src_ref=state_out.at[k],
-            dst_ref=state_in.at[k],
-            send_sem=state_send.at[k],
-            recv_sem=state_recv.at[k],
-            device_id={"seq": partners[k]},
+            dst_ref=state_in.at[slots[k, j]],
+            send_sem=state_send.at[slots[k, j]],
+            recv_sem=state_recv.at[slots[k, j]],
+            device_id={"seq": partners[k][j - 1]},
             device_id_type=MESH,
         )
 
@@ -242,23 +272,46 @@
     carried_ref[...] = jnp.zeros_like(carried_ref)
     for k in range(levels):
         state_out[k] = total_ref[...].astype(jnp.bfloat16)
-        copy = state_copy(k)
-        copy.start()
+        radix, size, digit = radices[k], sizes[k], digits[k]
+        final = k == levels - 1
+        copies = [state_copy(k, j) for j in range(1, radix)]
+        for j, copy in enumerate(copies, 1):
+            if final:
+                pl.when(digit + j < radix)(copy.start)
+            else:
+                copy.start()
         for work in beside.get(k, []):
             work()
-        copy.wait()
-        size = 1 << k
         inside = lax.rem(me, size)
-        upper = lax.rem(lax.div(me, size), 2) == 1
-        span = (rows * inside).astype(jnp.float32)
-        rate = rate_ref[...]
-        arrived = state_in[k].astype(jnp.float32)
-        carried_ref[...] += jnp.where(upper, jnp.exp(-rate * span) * arrived, 0.0)
-        if k < levels - 1:
-            own = total_ref[...]
-            early = jnp.where(upper, arrived, own)
-            late = jnp.where(upper, own, arrived)
-            total_ref[...] = late + jnp.exp(-rate * (rows * size)) * early
+        if not final:
+            ahead = (rows * size * (radix - 1 - digit)).astype(jnp.float32)
+            grown = jnp.exp(-rate_ref[...] * ahead) * total_ref[...]
+        for j, copy in enumerate(copies, 1):
+
+            def absorb(k=k, j=j, size=size, inside=inside):
+                span = (rows * (inside + size * (j - 1))).astype(jnp.float32)
+                carried_ref[...] += jnp.exp(-rate_ref[...] * span) * state_in[
+                    slots[k, j]
+                ].astype(jnp.float32)
+
+            if final:
+
+                def receive(copy=copy, absorb=absorb):
+                    copy.wait_recv()
+                    absorb()
+
+                pl.when(digit >= j)(receive)
+            else:
+                copy.wait_recv()
+                pl.when(digit >= j)(absorb)
+                ahead = (
+                    rows * size * (radix - 1 - lax.rem(digit - j + radix, radix))
+                ).astype(jnp.float32)
+                grown = grown + jnp.exp(-rate_ref[...] * ahead) * state_in[
+                    slots[k, j]
+                ].astype(jnp.float32)
+        if not final:
+            total_ref[...] = grown
 
     for h in range(halves):
         factor = half_of(factor_ref, h)
@@ -273,6 +326,13 @@
             return state
 
         lax.fori_loop(0, rows, across, start, unroll=8)
+
+    for k in range(levels):
+        for j in range(1, radices[k]):
+            if k == levels - 1:
+                pl.when(digits[k] + j < radices[k])(state_copy(k, j).wait_send)
+            else:
+                state_copy(k, j).wait_send()
 
     padded = squares_ref.shape[0]
     squares_ref[...] = jnp.zeros_like(squares_ref)
@@ -389,7 +449,9 @@
     rows, width = residual.shape
     poles = decay_rate.shape[0]
     groups = width // LANES
-    levels = seq_size.bit_length() - 1
+    radices = radices_of(seq_size)
+    levels = len(radices)
+    slots = sum(radices) - levels
     padded = -(-rows // LANES) * LANES
     f32, bf16 = jnp.float32, jnp.bfloat16
     by_channel = (poles, groups, LANES)
@@ -429,13 +491,13 @@
             pltpu.VMEM((8, width), f32),
             pltpu.VMEM((8, width), f32),
             pltpu.VMEM((levels,) + by_channel, bf16),
-            pltpu.VMEM((levels,) + by_channel, bf16),
+            pltpu.VMEM((slots,) + by_channel, bf16),
             pltpu.VMEM((padded, LANES), f32),
             pltpu.VMEM((8, padded), f32),
             pltpu.VMEM((chan_size - 1, 8, padded), f32),
             pltpu.SemaphoreType.DMA((2,)),
-            pltpu.SemaphoreType.DMA((levels,)),
-            pltpu.SemaphoreType.DMA((levels,)),
+            pltpu.SemaphoreType.DMA((slots,)),
+            pltpu.SemaphoreType.DMA((slots,)),
             pltpu.SemaphoreType.DMA((chan_size - 1,)),
             pltpu.SemaphoreType.DMA((chan_size - 1,)),
         ],

time: 26.7 us -> 22.8 us (0.85)
  the two profiles are of different devices: /device:TPU:0 before, /device:TPU:6 now
where the time goes in v3:
time: 22.8 us; the launch traced here: 22.6 us
  Pallas kernels  22 us (96%)
  between operations  0.64 us (3%)
    pallas_call x1, Pallas kernels, body(): pl.pallas_call(functools.partial(kernel, seq_size, chan_size), out_shape=...  19.9 us
    pallas_call x1, Pallas kernels, body(): pl.pallas_call(finish, out_shape=(whole, whole), in_specs=[hbm] * 3, out_...  2.05 us

profile of v3, /device:TPU:6, one launch (start us, length us, event | category | flops | bytes accessed | tf_op | source)
XLA Modules:
  0.0 22.6 jit_solution(14583121628100681807)
XLA Ops:
  0.6 19.9 %shard_map.104 = (bf16[128,2048]{1,0:T(8,128)(2,1)}, f32[128,128]{1,0:T(8,128)}) custom-call(bf16[128,2048]{1,0:T(8,128)(2,1)} %residual_hbm.1, bf16[128,2048]{1,0:T(8,128)(2,1)} %query_hbm.1, bf16[128,2048]{1,0:T(8,128)(2,1)} %key_hbm.1, bf16[128,2048]{1,0:T(8,128)(2,1)} %value_hbm.1, f32[3,3,2048]{2,1,0:T(4,128)} %filter_hbm.1, f32[16,2048]{1,0:T(8,128)} %decay_hbm.1, ...), custom_call_target="tpu_custom_call" | custom-call | tf_op jit(solution)/shard_map/pallas_call | solution.py:460
  20.6 2.0 %shard_map.105 = (bf16[128,2048]{1,0:T(8,128)(2,1)}, bf16[128,2048]{1,0:T(8,128)(2,1)}) custom-call(bf16[128,2048]{1,0:T(8,128)(2,1)} %get-tuple-element.4.summed_hbm, f32[128,128]{1,0:T(8,128)} %get-tuple-element.5.inverse_hbm, f32[1,2048]{1,0:T(1,128)} %bitcast.3), custom_call_target="tpu_custom_call" | custom-call | tf_op jit(solution)/shard_map/pallas_call | solution.py:518

commit v4 on v3

--- a/solution.py
+++ b/solution.py
@@ -171,9 +171,6 @@
         mix_ref[place_of(g, 2), :] = jnp.zeros((2, LANES), jnp.float32)
         return 0
 
-    for load in loads[5:8]:
-        load.wait()
-    lax.fori_loop(0, groups, mix_all, 0)
     for load in loads[:3]:
         load.wait()
     for i in range(3):
@@ -190,6 +187,9 @@
         device_id_type=MESH,
     )
     tail_copy.start()
+    for load in loads[5:8]:
+        load.wait()
+    lax.fori_loop(0, groups, mix_all, 0)
 
     def half_of(ref, h):
         return tuple(ref[p, h * 8 : h * 8 + 8, :] for p in range(poles))
@@ -350,8 +350,6 @@
         return 0
 
     lax.fori_loop(0, groups, gate, 0)
-    store_summed = pltpu.make_async_copy(summed_ref, summed_hbm, store_sem.at[0])
-    store_summed.start()
     row_squares = jnp.sum(jnp.transpose(squares_ref[...]), axis=0, keepdims=True)
     squares_out[...] = jnp.broadcast_to(row_squares, (8, padded))
     chan_copies = [
@@ -367,6 +365,8 @@
     ]
     for copy in chan_copies:
         copy.start()
+    store_summed = pltpu.make_async_copy(summed_ref, summed_hbm, store_sem.at[0])
+    store_summed.start()
     for copy in chan_copies:
         copy.wait()
     together = squares_out[...]

time: 22.8 us -> 21.7 us (0.952)
  the two profiles are of different devices: /device:TPU:6 before, /device:TPU:4 now
where the time goes in v4:
time: 21.7 us; the launch traced here: 21.6 us
  Pallas kernels  20.9 us (96%)
  between operations  0.64 us (3%)
    pallas_call x1, Pallas kernels, body(): pl.pallas_call(functools.partial(kernel, seq_size, chan_size), out_shape=...  18.9 us
    pallas_call x1, Pallas kernels, body(): pl.pallas_call(finish, out_shape=(whole, whole), in_specs=[hbm] * 3, out_...  2.05 us

profile of v4, /device:TPU:4, one launch (start us, length us, event | category | flops | bytes accessed | tf_op | source)
XLA Modules:
  0.0 21.6 jit_solution(17204168926178196998)
XLA Ops:
  0.6 18.9 %shard_map.104 = (bf16[128,2048]{1,0:T(8,128)(2,1)}, f32[128,128]{1,0:T(8,128)}) custom-call(bf16[128,2048]{1,0:T(8,128)(2,1)} %residual_hbm.1, bf16[128,2048]{1,0:T(8,128)(2,1)} %query_hbm.1, bf16[128,2048]{1,0:T(8,128)(2,1)} %key_hbm.1, bf16[128,2048]{1,0:T(8,128)(2,1)} %value_hbm.1, f32[3,3,2048]{2,1,0:T(4,128)} %filter_hbm.1, f32[16,2048]{1,0:T(8,128)} %decay_hbm.1, ...), custom_call_target="tpu_custom_call" | custom-call | tf_op jit(solution)/shard_map/pallas_call | solution.py:460
  19.5 2.0 %shard_map.105 = (bf16[128,2048]{1,0:T(8,128)(2,1)}, bf16[128,2048]{1,0:T(8,128)(2,1)}) custom-call(bf16[128,2048]{1,0:T(8,128)(2,1)} %get-tuple-element.4.summed_hbm, f32[128,128]{1,0:T(8,128)} %get-tuple-element.5.inverse_hbm, f32[1,2048]{1,0:T(1,128)} %bitcast.3), custom_call_target="tpu_custom_call" | custom-call | tf_op jit(solution)/shard_map/pallas_call | solution.py:518

commit v5 on v4

--- a/solution.py
+++ b/solution.py
@@ -189,7 +189,7 @@
     tail_copy.start()
     for load in loads[5:8]:
         load.wait()
-    lax.fori_loop(0, groups, mix_all, 0)
+    lax.fori_loop(0, groups, mix_all, 0, unroll=2)
 
     def half_of(ref, h):
         return tuple(ref[p, h * 8 : h * 8 + 8, :] for p in range(poles))
@@ -208,7 +208,7 @@
             current = mix_ref[token(h, t), :]
             return tuple(a * s + current for a, s in zip(factor, state))
 
-        state = lax.fori_loop(0, rows, advance, zeros, unroll=8)
+        state = lax.fori_loop(0, rows, advance, zeros, unroll=16)
         for p in range(poles):
             total_ref[p, h * 8 : h * 8 + 8, :] = state[p]
 
@@ -222,7 +222,7 @@
         mix_ref[place_of(g, 8), :] = product[0:8, :]
         return 0
 
-    lax.fori_loop(0, groups, mix_first, 0)
+    lax.fori_loop(0, groups, mix_first, 0, unroll=4)
 
     reach = jnp.exp(-rate_ref[...] * (rows - 2.0))
     total_ref[...] = total_ref[...] + reach * (factor_ref[...] * first_tokens(0) + first_tokens(1))
@@ -259,12 +259,12 @@
             )
             return state
 
-        lax.fori_loop(0, rows, advance, zeros, unroll=8)
+        lax.fori_loop(0, rows, advance, zeros, unroll=16)
 
     def query_work():
         for load in loads[8:]:
             load.wait()
-        lax.fori_loop(0, groups, query_all, 0)
+        lax.fori_loop(0, groups, query_all, 0, unroll=2)
 
     beside = {0: [query_work]}
     for h in range(halves):
@@ -325,7 +325,7 @@
             conv_ref[token(h, t), :] = conv_ref[token(h, t), :] + tree_sum(list(state))
             return state
 
-        lax.fori_loop(0, rows, across, start, unroll=8)
+        lax.fori_loop(0, rows, across, start, unroll=16)
 
     for k in range(levels):
         for j in range(1, radices[k]):
@@ -349,7 +349,7 @@
         squares_ref[0:rows, :] += widened * widened
         return 0
 
-    lax.fori_loop(0, groups, gate, 0)
+    lax.fori_loop(0, groups, gate, 0, unroll=2)
     row_squares = jnp.sum(jnp.transpose(squares_ref[...]), axis=0, keepdims=True)
     squares_out[...] = jnp.broadcast_to(row_squares, (8, padded))
     chan_copies = [

time: 21.7 us -> 21.6 us (level)
  no operation moved by 1% of the time
where the time goes in v5:
time: 21.6 us; the launch traced here: 21.4 us
  Pallas kernels  20.8 us (96%)
  between operations  0.64 us (3%)
    pallas_call x1, Pallas kernels, body(): pl.pallas_call(functools.partial(kernel, seq_size, chan_size), out_shape=...  18.7 us
    pallas_call x1, Pallas kernels, body(): pl.pallas_call(finish, out_shape=(whole, whole), in_specs=[hbm] * 3, out_...  2.05 us

profile of v5, /device:TPU:4, one launch (start us, length us, event | category | flops | bytes accessed | tf_op | source)
XLA Modules:
  0.0 21.4 jit_solution(15415416507606709130)
XLA Ops:
  0.6 18.7 %shard_map.104 = (bf16[128,2048]{1,0:T(8,128)(2,1)}, f32[128,128]{1,0:T(8,128)}) custom-call(bf16[128,2048]{1,0:T(8,128)(2,1)} %residual_hbm.1, bf16[128,2048]{1,0:T(8,128)(2,1)} %query_hbm.1, bf16[128,2048]{1,0:T(8,128)(2,1)} %key_hbm.1, bf16[128,2048]{1,0:T(8,128)(2,1)} %value_hbm.1, f32[3,3,2048]{2,1,0:T(4,128)} %filter_hbm.1, f32[16,2048]{1,0:T(8,128)} %decay_hbm.1, ...), custom_call_target="tpu_custom_call" | custom-call | tf_op jit(solution)/shard_map/pallas_call | solution.py:460
  19.4 2.0 %shard_map.105 = (bf16[128,2048]{1,0:T(8,128)(2,1)}, bf16[128,2048]{1,0:T(8,128)(2,1)}) custom-call(bf16[128,2048]{1,0:T(8,128)(2,1)} %get-tuple-element.4.summed_hbm, f32[128,128]{1,0:T(8,128)} %get-tuple-element.5.inverse_hbm, f32[1,2048]{1,0:T(1,128)} %bitcast.3), custom_call_target="tpu_custom_call" | custom-call | tf_op jit(solution)/shard_map/pallas_call | solution.py:518
